TPU v7x, 32 devices: a whole 2x2x4 slice. The times are simulated.
32 devices in a mesh: fsdp: 4 (over z), context: 2 (over y), tensor: 4 (over x, core).
Axes of the slice: x: 2, y: 2, z: 4, core: 2. Of those that a mesh axis runs over, the one named last changes fastest.
Arguments:
- tokens: bfloat16 [8, 4096, 768], P('fsdp', 'context'), may hold values from -6 to 6
- cotangent: bfloat16 [8, 4096, 768], P('fsdp', 'context'), may hold values from -6 to 6
- segments: int32 [8, 4096], P('fsdp'), may hold values from 0 to 4, as said below
- steps: int32 [8], P('fsdp'), may hold values from 0 to 255
- table: bfloat16 [256, 128], replicated, may hold values from -5 to 5
- ada_w: bfloat16 [128, 4608], replicated, may hold values from -0.5 to 0.5
- ada_b: bfloat16 [4608], replicated, may hold values from 0.099609375 to 1.8984375
- gain_one: bfloat16 [768], replicated, may hold values from 0.099609375 to 1.8984375
- w_qkv: bfloat16 [768, 2304], P('fsdp', 'tensor'), may hold values from -0.109375 to 0.109375
- w_out: bfloat16 [768, 768], P('tensor', 'fsdp'), may hold values from -3 to 3
- gain_two: bfloat16 [768], replicated, may hold values from 0.099609375 to 1.8984375
- w_up: bfloat16 [768, 3072], P('fsdp', 'tensor'), may hold values from -0.109375 to 0.109375
- b_up: bfloat16 [3072], replicated, may hold values from -3 to 3
- w_down: bfloat16 [3072, 768], P('tensor', 'fsdp'), may hold values from -0.15625 to 0.15625
- b_down: bfloat16 [768], replicated, may hold values from -3 to 3
Outputs:
- block_out: bfloat16 [8, 4096, 768], P('fsdp', 'context')
- grad_tokens: float32 [8, 4096, 768], P('fsdp', 'context', 'tensor')
- grad_table: float32 [256, 128], replicated
- grad_ada_w: float32 [128, 4608], replicated
- grad_ada_b: float32 [4608], replicated
- grad_gain_one: float32 [768], replicated
- grad_w_qkv: float32 [768, 2304], P('fsdp', 'tensor')
- grad_w_out: float32 [768, 768], P('tensor', 'fsdp')
- grad_gain_two: float32 [768], replicated
- grad_w_up: float32 [768, 3072], P('fsdp', 'tensor')
- grad_b_up: float32 [3072], replicated
- grad_w_down: float32 [3072, 768], P('tensor', 'fsdp')
- grad_b_down: float32 [768], replicated
Inputs may be any that keep to these rules, and one draw needn't show every extreme that they name: `segments`: along each sequence segment numbers never fall; 1 to 4 are its documents in order, each present, and 0 marks the padding at its end, present in every sequence. No document has more than 2048 tokens, and in every sequence one document has exactly 2048.
All inputs are finite; a program needn't handle non-finite values.
Results may differ from a plain program's by a relative error of at most 0.02.
Values may be sent and summed in bfloat16 or wider, within the bound.
A program may use at most 768 MiB of HBM per device.

v0:
```python
from functools import partial
import jax
import jax.numpy as jnp
from jax import lax
from jax.sharding import PartitionSpec as P

HDIM = 64
precise = lax.Precision.HIGHEST


def product(left_side, right_side):
    return jnp.dot(left_side, right_side, preferred_element_type=jnp.float32)


def transposed(left_side, right_side):
    return lax.dot_general(
        left_side, right_side, (((0,), (0,)), ((), ())), preferred_element_type=jnp.float32
    )


def against(left_side, right_side):
    return lax.dot_general(
        left_side, right_side, (((1,), (1,)), ((), ())), preferred_element_type=jnp.float32
    )


def exact_product(left_side, right_side):
    return jnp.dot(left_side, right_side, precision=precise, preferred_element_type=jnp.float32)


def exact_transposed(left_side, right_side):
    return lax.dot_general(
        left_side,
        right_side,
        (((0,), (0,)), ((), ())),
        precision=precise,
        preferred_element_type=jnp.float32,
    )


def exact_against(left_side, right_side):
    return lax.dot_general(
        left_side,
        right_side,
        (((1,), (1,)), ((), ())),
        precision=precise,
        preferred_element_type=jnp.float32,
    )


def normalize(operand):
    center = operand - jnp.mean(operand, axis=-1, keepdims=True)
    scaling = lax.rsqrt(jnp.mean(center * center, axis=-1, keepdims=True) + 1e-05)
    return (center * scaling, scaling)


def norm_back(grad_hat, hatted, scaling):
    return scaling * (
        grad_hat
        - jnp.mean(grad_hat, axis=-1, keepdims=True)
        - hatted * jnp.mean(grad_hat * hatted, axis=-1, keepdims=True)
    )


def positions(segment):
    indices = jnp.arange(segment.shape[0], dtype=jnp.int32)
    change = jnp.concatenate([jnp.ones((1,), jnp.bool_), segment[1:] != segment[:-1]])
    starts = lax.cummax(jnp.where(change, indices, 0), axis=0)
    return indices - starts


def angles_of(offsets, half_width):
    frequency = 10000.0 ** (-jnp.arange(half_width, dtype=jnp.float32) / half_width)
    angles = offsets.astype(jnp.float32)[:, None] * frequency[None, :]
    return (jnp.cos(angles)[:, None, :], jnp.sin(angles)[:, None, :])


def rotate(operand, cosine, sine_part, direction):
    half_width = operand.shape[-1] // 2
    front_half = operand[..., :half_width]
    second = operand[..., half_width:]
    return jnp.concatenate(
        [
            front_half * cosine - direction * second * sine_part,
            direction * front_half * sine_part + second * cosine,
        ],
        axis=-1,
    )


def scores_of(queries, key_rows, allowed):
    raw_scores = (
        jnp.einsum("qhd,khd->hqk", queries, key_rows, preferred_element_type=jnp.float32) * 0.125
    )
    return jnp.where(allowed[None], raw_scores, -1e30)


def attend(queries, key_rows, values, allowed):
    scores = scores_of(queries, key_rows, allowed)
    row_max = jnp.max(scores, axis=-1, keepdims=True)
    weights_raw = jnp.exp(scores - row_max)
    row_total = jnp.sum(weights_raw, axis=-1, keepdims=True)
    weights_low = (weights_raw / row_total).astype(jnp.bfloat16)
    mixture = jnp.einsum("hqk,khd->qhd", weights_low, values, preferred_element_type=jnp.float32)
    return (mixture, row_max + jnp.log(row_total))


def attend_back(queries, key_rows, values, grad_mixture, logsum, allowed, row_delta):
    scores = scores_of(queries, key_rows, allowed)
    chances = jnp.exp(scores - logsum)
    grad_chances = jnp.einsum(
        "qhd,khd->hqk", grad_mixture, values, preferred_element_type=jnp.float32
    )
    row_delta = jnp.sum(chances * grad_chances, axis=-1, keepdims=True)
    grad_scores = (chances * (grad_chances - row_delta)).astype(jnp.bfloat16)
    return (chances.astype(jnp.bfloat16), grad_scores, row_delta)


def local(
    tokens,
    cotangent,
    segments,
    steps,
    table,
    ada_w,
    ada_b,
    gain_one,
    w_qkv,
    w_out,
    gain_two,
    w_up,
    b_up,
    w_down,
    b_down,
):
    w_qkv, w_up, w_out, w_down = (
        lax.all_gather(w_qkv, "fsdp", axis=0, tiled=True),
        lax.all_gather(w_up, "fsdp", axis=0, tiled=True),
        lax.all_gather(w_out, "fsdp", axis=1, tiled=True),
        lax.all_gather(w_down, "fsdp", axis=1, tiled=True),
    )
    tensor_rank = lax.axis_index("tensor")
    context_rank = lax.axis_index("context")
    sequences, own_rows, model_width = tokens.shape
    length = segments.shape[1]
    local_heads = w_out.shape[0] // HDIM
    hidden_width = w_up.shape[1]
    up_bias = lax.dynamic_slice_in_dim(b_up, tensor_rank * hidden_width, hidden_width).astype(
        jnp.float32
    )
    down_bias = b_down.astype(jnp.float32)
    gain_first = gain_one.astype(jnp.float32)
    gain_second = gain_two.astype(jnp.float32)
    leader = (tensor_rank == 0).astype(jnp.float32)
    ada_full = ada_w.astype(jnp.float32)
    choose = (steps[:, None] == jnp.arange(table.shape[0], dtype=jnp.int32)[None, :]).astype(
        jnp.float32
    )
    before = exact_product(choose, table.astype(jnp.float32))
    embedding, silu_back = jax.vjp(jax.nn.silu, before)
    modulation = exact_product(embedding, ada_full) + ada_b.astype(jnp.float32)
    grad_qkv = jnp.zeros(w_qkv.shape, jnp.float32)
    grad_out_w = jnp.zeros(w_out.shape, jnp.float32)
    grad_up = jnp.zeros(w_up.shape, jnp.float32)
    grad_down = jnp.zeros(w_down.shape, jnp.float32)
    grad_bias_up = jnp.zeros((hidden_width,), jnp.float32)
    grad_bias_down = jnp.zeros((model_width,), jnp.float32)
    grad_gain_first = jnp.zeros((model_width,), jnp.float32)
    grad_gain_second = jnp.zeros((model_width,), jnp.float32)
    results = []
    partial_inputs = []
    carried = []
    grad_mods = []
    for number in range(sequences):
        shift_one, scale_one, gate_one, shift_two, scale_two, gate_two = jnp.split(
            modulation[number], 6
        )
        segment = segments[number]
        offsets = positions(segment)
        own_segment = lax.dynamic_slice_in_dim(segment, context_rank * own_rows, own_rows)
        own_offsets = lax.dynamic_slice_in_dim(offsets, context_rank * own_rows, own_rows)
        cosine, sine_part = angles_of(own_offsets, HDIM // 2)
        allowed = own_segment[:, None] == segment[None, :]
        inputs_row = tokens[number].astype(jnp.float32)
        hat_one, scaling_one = normalize(inputs_row)
        lifted_one = hat_one * gain_first
        entry_one = (lifted_one * (1.0 + scale_one) + shift_one).astype(jnp.bfloat16)
        projected = product(entry_one, w_qkv).reshape(own_rows, local_heads, 3, HDIM)
        queries = rotate(projected[:, :, 0], cosine, sine_part, 1.0).astype(jnp.bfloat16)
        key_rows = rotate(projected[:, :, 1], cosine, sine_part, 1.0).astype(jnp.bfloat16)
        values = projected[:, :, 2].astype(jnp.bfloat16)
        key_value = jnp.stack([key_rows, values], axis=1).reshape(own_rows, 2 * local_heads * HDIM)
        gathered = lax.all_gather(key_value, "context", axis=0, tiled=True).reshape(
            length, 2, local_heads, HDIM
        )
        all_keys = gathered[:, 0]
        all_values = gathered[:, 1]
        mixture, logsum = attend(queries, all_keys, all_values, allowed)
        mixture_low = mixture.reshape(own_rows, local_heads * HDIM).astype(jnp.bfloat16)
        attended = lax.psum(product(mixture_low, w_out).astype(jnp.bfloat16), "tensor").astype(
            jnp.float32
        )
        middle = inputs_row + gate_one * attended
        hat_two, scaling_two = normalize(middle)
        lifted_two = hat_two * gain_second
        entry_two = (lifted_two * (1.0 + scale_two) + shift_two).astype(jnp.bfloat16)
        hidden = product(entry_two, w_up) + up_bias
        activated, gelu_back = jax.vjp(partial(jax.nn.gelu, approximate=True), hidden)
        activated_low = activated.astype(jnp.bfloat16)
        output = (
            lax.psum(product(activated_low, w_down).astype(jnp.bfloat16), "tensor").astype(
                jnp.float32
            )
            + down_bias
        )
        results.append((middle + gate_two * output).astype(jnp.bfloat16))
        valid = (own_segment != 0).astype(jnp.float32)[:, None]
        grad_result = cotangent[number].astype(jnp.float32) * valid
        grad_output = (gate_two * grad_result).astype(jnp.bfloat16)
        grad_gate_two = jnp.sum(grad_result * output, axis=0)
        grad_bias_down = grad_bias_down + jnp.sum(grad_output.astype(jnp.float32), axis=0)
        grad_down = grad_down + transposed(activated_low, grad_output)
        grad_active = against(grad_output, w_down)
        grad_hidden = gelu_back(grad_active)[0].astype(jnp.bfloat16)
        grad_bias_up = grad_bias_up + jnp.sum(grad_hidden.astype(jnp.float32), axis=0)
        grad_up = grad_up + transposed(entry_two, grad_hidden)
        grad_entry_two = against(grad_hidden, w_up)
        grad_shift_two = jnp.sum(grad_entry_two, axis=0)
        grad_scale_two = jnp.sum(grad_entry_two * lifted_two, axis=0)
        grad_lifted_two = grad_entry_two * (1.0 + scale_two)
        grad_gain_second = grad_gain_second + jnp.sum(grad_lifted_two * hat_two, axis=0)
        part_two = norm_back(grad_lifted_two * gain_second, hat_two, scaling_two)
        grad_middle = grad_result + lax.psum(part_two.astype(jnp.bfloat16), "tensor").astype(
            jnp.float32
        )
        grad_attended = (gate_one * grad_middle).astype(jnp.bfloat16)
        grad_gate_one = jnp.sum(grad_middle * attended, axis=0)
        grad_out_w = grad_out_w + transposed(mixture_low, grad_attended)
        grad_mixture = (
            against(grad_attended, w_out).astype(jnp.bfloat16).reshape(own_rows, local_heads, HDIM)
        )
        chances_low, grad_scores, row_delta = attend_back(
            queries, all_keys, all_values, grad_mixture, logsum, allowed, None
        )
        grad_queries = (
            jnp.einsum("hqk,khd->qhd", grad_scores, all_keys, preferred_element_type=jnp.float32)
            * 0.125
        )
        grad_all_keys = (
            jnp.einsum("hqk,qhd->khd", grad_scores, queries, preferred_element_type=jnp.float32)
            * 0.125
        )
        grad_all_values = jnp.einsum(
            "hqk,qhd->khd", chances_low, grad_mixture, preferred_element_type=jnp.float32
        )
        both_grads = jnp.stack([grad_all_keys, grad_all_values], axis=1).reshape(
            length, 2 * local_heads * HDIM
        )
        own_grads = (
            lax.psum_scatter(
                both_grads.astype(jnp.bfloat16), "context", scatter_dimension=0, tiled=True
            )
            .astype(jnp.float32)
            .reshape(own_rows, 2, local_heads, HDIM)
        )
        grad_keys = own_grads[:, 0]
        grad_values = own_grads[:, 1]
        grad_queries = rotate(grad_queries, cosine, sine_part, -1.0)
        grad_keys = rotate(grad_keys, cosine, sine_part, -1.0)
        grad_projected = (
            jnp.stack([grad_queries, grad_keys, grad_values], axis=2)
            .reshape(own_rows, local_heads * 3 * HDIM)
            .astype(jnp.bfloat16)
        )
        grad_qkv = grad_qkv + transposed(entry_one, grad_projected)
        grad_entry_one = against(grad_projected, w_qkv)
        grad_shift_one = jnp.sum(grad_entry_one, axis=0)
        grad_scale_one = jnp.sum(grad_entry_one * lifted_one, axis=0)
        grad_lifted_one = grad_entry_one * (1.0 + scale_one)
        grad_gain_first = grad_gain_first + jnp.sum(grad_lifted_one * hat_one, axis=0)
        partial_inputs.append(norm_back(grad_lifted_one * gain_first, hat_one, scaling_one))
        carried.append(grad_middle)
        grad_mods.append(
            jnp.concatenate(
                [
                    grad_shift_one,
                    grad_scale_one,
                    grad_gate_one * leader,
                    grad_shift_two,
                    grad_scale_two,
                    grad_gate_two * leader,
                ]
            )
        )
    summed_inputs = lax.psum_scatter(
        jnp.stack(partial_inputs).astype(jnp.bfloat16), "tensor", scatter_dimension=2, tiled=True
    ).astype(jnp.float32)
    slice_width = model_width // lax.axis_size("tensor")
    own_middle = lax.dynamic_slice_in_dim(
        jnp.stack(carried), tensor_rank * slice_width, slice_width, axis=2
    )
    grad_tokens = summed_inputs + own_middle
    grad_mod = jnp.stack(grad_mods)
    bias_up_full = lax.dynamic_update_slice_in_dim(
        jnp.zeros((b_up.shape[0],), jnp.float32), grad_bias_up, tensor_rank * hidden_width, 0
    )
    grad_qkv, grad_up, grad_out_w, grad_down = (
        lax.psum_scatter(
            grad_qkv.astype(jnp.bfloat16), "fsdp", scatter_dimension=0, tiled=True
        ).astype(jnp.float32),
        lax.psum_scatter(
            grad_up.astype(jnp.bfloat16), "fsdp", scatter_dimension=0, tiled=True
        ).astype(jnp.float32),
        lax.psum_scatter(
            grad_out_w.astype(jnp.bfloat16), "fsdp", scatter_dimension=1, tiled=True
        ).astype(jnp.float32),
        lax.psum_scatter(
            grad_down.astype(jnp.bfloat16), "fsdp", scatter_dimension=1, tiled=True
        ).astype(jnp.float32),
    )
    grad_qkv, grad_up, grad_out_w, grad_down = (
        lax.psum(grad_qkv.astype(jnp.bfloat16), "context").astype(jnp.float32),
        lax.psum(grad_up.astype(jnp.bfloat16), "context").astype(jnp.float32),
        lax.psum(grad_out_w.astype(jnp.bfloat16), "context").astype(jnp.float32),
        lax.psum(grad_down.astype(jnp.bfloat16), "context").astype(jnp.float32),
    )
    grad_ada_b = jnp.sum(grad_mod, axis=0)
    grad_ada_w = exact_transposed(embedding, grad_mod)
    grad_embedding = exact_against(grad_mod, ada_full)
    grad_before = silu_back(grad_embedding)[0]
    grad_table = exact_transposed(choose, grad_before)
    (
        grad_table,
        grad_ada_w,
        grad_ada_b,
        grad_gain_first,
        grad_gain_second,
        bias_up_full,
        grad_bias_down,
    ) = lax.psum(
        (
            grad_table,
            grad_ada_w,
            grad_ada_b,
            grad_gain_first,
            grad_gain_second,
            bias_up_full,
            grad_bias_down * leader,
        ),
        ("fsdp", "context", "tensor"),
    )
    return (
        jnp.stack(results),
        grad_tokens,
        grad_table,
        grad_ada_w,
        grad_ada_b,
        grad_gain_first,
        grad_qkv,
        grad_out_w,
        grad_gain_second,
        grad_up,
        bias_up_full,
        grad_down,
        grad_bias_down,
    )


def solution(mesh):
    return jax.shard_map(
        local,
        mesh=mesh,
        in_specs=(
            P("fsdp", "context", None),
            P("fsdp", "context", None),
            P("fsdp", None),
            P("fsdp"),
            P(),
            P(),
            P(),
            P(),
            P("fsdp", "tensor"),
            P("tensor", "fsdp"),
            P(),
            P("fsdp", "tensor"),
            P(),
            P("tensor", "fsdp"),
            P(),
        ),
        out_specs=(
            P("fsdp", "context", None),
            P("fsdp", "context", "tensor"),
            P(),
            P(),
            P(),
            P(),
            P("fsdp", "tensor"),
            P("tensor", "fsdp"),
            P(),
            P("fsdp", "tensor"),
            P(),
            P("tensor", "fsdp"),
            P(),
        ),
        check_vma=False,
    )
```

profile of v0, /device:TPU:0, one launch (start us, length us, event | category | flops | bytes accessed | tf_op | source)
XLA Modules:
  0.0 1699.0 jit_solution(8537734256310967718)
XLA Ops:
  17.1 23.5 %all_gather.18 = bf16[768,576]{1,0:T(8,128)(2,1)S(1)} all-gather(bf16[192,576]{1,0:T(8,128)(2,1)S(1)} %copy-done.39), channel_id=1, replica_groups=mesh['fsdp'=4,'context'=2,'tensor'=4] {'fsdp'}, dimensions={0}, use_global_device_ids=true | all-gather | bytes 1105920 | tf_op jit(solution)/shard_map/all_gather | solution.py:137
  113.9 37.9 %fusion.185 = (f32[3,2048]{1,0:T(4,128)S(1)}, f32[3,2048,4096]{2,1,0:T(8,128)}) fusion(bf16[4096,2,3,64]{0,3,2,1:T(8,128)(2,1)} %bitcast.367, bf16[2048,3,32]{0,2,1:T(8,128)(2,1)S(1)} %get-tuple-element.152, bf16[2048,3,32]{0,2,1:T(8,128)(2,1)S(1)} %get-tuple-element.151, pred[2048,4096]{1,0:T(8,128)(4,1)} %broadcast_compare_fusion.1), kind=kOutput, calls=%fused_computation.352 | convolution fusion | flops 3298289664 | bytes 111435776 | tf_op jit(solution)/shard_map/qhd,khd->hqk/dot_general | solution.py:93
  151.9 31.0 %fusion = f32[3,2048]{1,0:T(4,128)S(1)} fusion(f32[3,2048,4096]{2,1,0:T(8,128)} %get-tuple-element.175, f32[3,2048]{1,0:T(4,128)S(1)} %get-tuple-element.174), kind=kLoop, calls=%fused_computation.12 | loop fusion | flops 50325504 | bytes 100712448 | tf_op jit(solution)/shard_map/reduce_sum | solution.py:102
  182.9 33.9 %fusion.119 = bf16[3,64,2048]{2,1,0:T(8,128)(2,1)S(1)} fusion(f32[3,2048,4096]{2,1,0:T(8,128)} %get-tuple-element.175, f32[3,2048]{1,0:T(4,128)S(1)} %fusion, f32[3,2048]{1,0:T(4,128)S(1)} %get-tuple-element.174, bf16[4096,2,3,64]{0,3,2,1:T(8,128)(2,1)} %bitcast.368), kind=kOutput, calls=%fused_computation.184 | convolution fusion | flops 3297116160 | bytes 103071744 | tf_op jit(solution)/shard_map/hqk,khd->qhd/dot_general | solution.py:104
  219.7 68.5 %all-reduce.13.cloned.1.call-done = bf16[2048,768]{1,0:T(8,128)(2,1)} async-done(((bf16[2048,768]{1,0:T(8,128)(2,1)}), bf16[2048,768]{1,0:T(8,128)(2,1)}) %all-reduce.13.cloned.1.call-update) | async-done | bytes 3145744 | tf_op jit(solution)/shard_map/psum | solution.py:200
  309.3 35.7 %all-gather.11.cloned.1.call-done = bf16[4096,384]{0,1:T(8,128)(2,1)} async-done(((bf16[2048,384]{0,1:T(8,128)(2,1)}), bf16[4096,384]{0,1:T(8,128)(2,1)}) %all-gather.11.cloned.1.call-update) | async-done | bytes 3145744 | tf_op jit(solution)/shard_map/all_gather | solution.py:193
  345.0 37.4 %fusion.186 = (f32[3,2048]{1,0:T(4,128)S(1)}, f32[3,2048,4096]{2,1,0:T(8,128)}) fusion(bf16[4096,2,3,64]{0,3,2,1:T(8,128)(2,1)} %bitcast.371, bf16[2048,3,32]{0,2,1:T(8,128)(2,1)S(1)} %get-tuple-element.148, bf16[2048,3,32]{0,2,1:T(8,128)(2,1)S(1)} %get-tuple-element.147, pred[2048,4096]{1,0:T(8,128)(4,1)} %broadcast_compare_fusion), kind=kOutput, calls=%fused_computation.353 | convolution fusion | flops 3298289664 | bytes 111435776 | tf_op jit(solution)/shard_map/qhd,khd->hqk/dot_general | solution.py:93
  382.4 31.0 %fusion.1 = f32[3,2048]{1,0:T(4,128)S(1)} fusion(f32[3,2048,4096]{2,1,0:T(8,128)} %get-tuple-element.177, f32[3,2048]{1,0:T(4,128)S(1)} %get-tuple-element.176), kind=kLoop, calls=%fused_computation.13 | loop fusion | flops 50325504 | bytes 100712448 | tf_op jit(solution)/shard_map/reduce_sum | solution.py:102
  413.5 34.5 %fusion.118 = bf16[3,64,2048]{2,1,0:T(8,128)(2,1)} fusion(f32[3,2048,4096]{2,1,0:T(8,128)} %get-tuple-element.177, f32[3,2048]{1,0:T(4,128)S(1)} %fusion.1, f32[3,2048]{1,0:T(4,128)S(1)} %get-tuple-element.176, bf16[4096,2,3,64]{0,3,2,1:T(8,128)(2,1)} %bitcast.372), kind=kOutput, calls=%fused_computation.183 | convolution fusion | flops 3297116160 | bytes 103071744 | tf_op jit(solution)/shard_map/hqk,khd->qhd/dot_general | solution.py:104
  454.3 66.5 %all-reduce.15.cloned.1.call-done = bf16[2048,768]{1,0:T(8,128)(2,1)} async-done(((bf16[2048,768]{1,0:T(8,128)(2,1)}), bf16[2048,768]{1,0:T(8,128)(2,1)}) %all-reduce.15.cloned.1.call-update) | async-done | bytes 3145744 | tf_op jit(solution)/shard_map/psum | solution.py:200
  586.1 118.6 %all-reduce.21.cloned.1.call-done = (bf16[2048,768]{1,0:T(8,128)(2,1)}, bf16[2048,768]{1,0:T(8,128)(2,1)}) async-done(((bf16[2048,768]{1,0:T(8,128)(2,1)}, bf16[2048,768]{1,0:T(8,128)(2,1)}), (bf16[2048,768]{1,0:T(8,128)(2,1)}, bf16[2048,768]{1,0:T(8,128)(2,1)})) %all-reduce.21.cloned.1.call-update) | async-done | bytes 6291472 | tf_op jit(solution)/shard_map/psum | solution.py:233
  714.6 33.7 %fusion.86 = bf16[4096,1,3,64]{0,3,2,1:T(8,128)(2,1)} fusion(bf16[2048,3,64]{0,2,1:T(8,128)(2,1)S(1)} %bitcast.365, f32[3,2048,4096]{2,1,0:T(8,128)} %get-tuple-element.177, f32[3,2048]{1,0:T(4,128)S(1)} %log_add_fusion), kind=kOutput, calls=%fused_computation.145 | convolution fusion | flops 3272343552 | bytes 103047168 | tf_op jit(solution)/shard_map/hqk,qhd->khd/dot_general | solution.py:253
  748.4 65.7 %multiply_reduce_fusion = (f32[3,2048]{1,0:T(4,128)}, f32[3,2048,4096]{2,1,0:T(8,128)}) fusion(f32[3,2048,4096]{2,1,0:T(8,128)} %get-tuple-element.177, f32[3,2048]{1,0:T(4,128)} %copy-done.19, bf16[2048,3,64]{0,2,1:T(8,128)(2,1)S(1)} %bitcast.366, bf16[4096,2,3,64]{0,3,2,1:T(8,128)(2,1)} %bitcast.373), kind=kOutput, calls=%fused_computation.1 | convolution fusion | flops 3296716800 | bytes 203743232 | tf_op jit(solution)/shard_map/qhd,khd->hqk/dot_general | solution.py:111
  820.5 77.9 %multiply_convert_fusion = bf16[3,2048,4096]{2,1,0:T(8,128)(2,1)} fusion(f32[3,2048,4096]{2,1,0:T(8,128)} %get-tuple-element.184, f32[3,2048,4096]{2,1,0:T(8,128)} %get-tuple-element.177, f32[3,2048]{1,0:T(4,128)S(1)} %copy-done.45, f32[3,2048]{1,0:T(4,128)S(1)} %copy-done.20), kind=kLoop, calls=%fused_computation | loop fusion | flops 100663296 | bytes 251707392 | tf_op jit(solution)/shard_map/convert_element_type | solution.py:115
  898.3 21.3 %fusion.99 = bf16[4096,1,3,64]{0,3,2,1:T(8,128)(2,1)} fusion(bf16[3,2048,4096]{2,1,0:T(8,128)(2,1)} %multiply_convert_fusion, bf16[2048,3,32]{0,2,1:T(8,128)(2,1)S(1)} %copy-done.33, bf16[2048,3,32]{0,2,1:T(8,128)(2,1)S(1)} %copy-done.31), kind=kOutput, calls=%fused_computation.157 | convolution fusion | flops 3224371200 | bytes 52690944 | tf_op jit(solution)/shard_map/hqk,qhd->khd/dot_general | solution.py:250
  926.6 66.3 %multiply_reduce_fusion.1 = (f32[3,2048]{1,0:T(4,128)S(1)}, f32[3,2048,4096]{2,1,0:T(8,128)}) fusion(f32[3,2048,4096]{2,1,0:T(8,128)} %get-tuple-element.175, f32[3,2048]{1,0:T(4,128)S(1)} %copy-done.18, bf16[2048,3,64]{0,2,1:T(8,128)(2,1)S(1)} %bitcast.363, bf16[4096,2,3,64]{0,3,2,1:T(8,128)(2,1)} %bitcast.369), kind=kOutput, calls=%fused_computation.4 | convolution fusion | flops 3296716800 | bytes 203735040 | tf_op jit(solution)/shard_map/qhd,khd->hqk/dot_general | solution.py:111
  992.9 77.8 %multiply_convert_fusion.1 = bf16[3,2048,4096]{2,1,0:T(8,128)(2,1)} fusion(f32[3,2048,4096]{2,1,0:T(8,128)} %get-tuple-element.182, f32[3,2048,4096]{2,1,0:T(8,128)} %get-tuple-element.175, f32[3,2048]{1,0:T(4,128)S(1)} %get-tuple-element.181, f32[3,2048]{1,0:T(4,128)S(1)} %copy-done.18), kind=kLoop, calls=%fused_computation.3 | loop fusion | flops 100663296 | bytes 251707392 | tf_op jit(solution)/shard_map/convert_element_type | solution.py:115
  1070.7 21.2 %fusion.101 = bf16[4096,1,3,64]{0,3,2,1:T(8,128)(2,1)} fusion(bf16[3,2048,4096]{2,1,0:T(8,128)(2,1)} %multiply_convert_fusion.1, bf16[2048,3,32]{0,2,1:T(8,128)(2,1)S(1)} %copy-done.29, bf16[2048,3,32]{0,2,1:T(8,128)(2,1)S(1)} %copy-done.27), kind=kOutput, calls=%fused_computation.160 | convolution fusion | flops 3224371200 | bytes 52690944 | tf_op jit(solution)/shard_map/hqk,qhd->khd/dot_general | solution.py:250
  1091.9 32.6 %fusion.89 = bf16[4096,1,3,64]{0,3,2,1:T(8,128)(2,1)S(1)} fusion(bf16[2048,3,64]{0,2,1:T(8,128)(2,1)S(1)} %bitcast.364, f32[3,2048,4096]{2,1,0:T(8,128)} %get-tuple-element.175, f32[3,2048]{1,0:T(4,128)S(1)} %copy-done.18), kind=kOutput, calls=%fused_computation.146 | convolution fusion | flops 3272343552 | bytes 103047168 | tf_op jit(solution)/shard_map/hqk,qhd->khd/dot_general | solution.py:253
  1168.8 22.7 %fusion.120 = f32[2048,3,64]{0,2,1:T(8,128)} fusion(bf16[3,2048,4096]{2,1,0:T(8,128)(2,1)} %multiply_convert_fusion, bf16[4096,2,3,64]{0,3,2,1:T(8,128)(2,1)} %bitcast.374), kind=kOutput, calls=%fused_computation.190 | convolution fusion | flops 3221618688 | bytes 53477376 | tf_op jit(solution)/shard_map/hqk,khd->qhd/dot_general | solution.py:246
  1191.6 22.0 %fusion.121 = f32[2048,3,64]{0,2,1:T(8,128)S(1)} fusion(bf16[3,2048,4096]{2,1,0:T(8,128)(2,1)} %multiply_convert_fusion.1, bf16[4096,2,3,64]{0,3,2,1:T(8,128)(2,1)} %bitcast.370), kind=kOutput, calls=%fused_computation.192 | convolution fusion | flops 3221618688 | bytes 53477376 | tf_op jit(solution)/shard_map/hqk,khd->qhd/dot_general | solution.py:246
  1308.1 218.1 %all-reduce.19.cloned.1.call-done = (bf16[2048,768]{1,0:T(8,128)(2,1)}, bf16[2048,768]{1,0:T(8,128)(2,1)}, bf16[2,2048,768]{1,0,2:T(2,128)(2,1)}) async-done(((bf16[2048,768]{1,0:T(8,128)(2,1)}, bf16[2048,768]{1,0:T(8,128)(2,1)}, bf16[2,2048,768]{1,0,2:T(2,128)(2,1)}), (bf16[2048,768]{1,0:T(8,128)(2,1)}, bf16[2048,768]{1,0:T(8,128)(2,1)}, bf16[2,2048,768]{1,0,2:T(2,128)(2,1)})) %all-reduce.19.cloned.1.call-update) | async-done | bytes 12582928 | tf_op jit(solution)/shard_map/psum | solution.py:211
  1569.5 41.0 %all-reduce.1 = (f32[4608]{0:T(1024)}, f32[768]{0:T(1024)}, f32[768]{0:T(1024)}, f32[3072]{0:T(1024)}, f32[768]{0:T(1024)}) all-reduce(f32[4608]{0:T(1024)S(1)} %reduce_sum.399, f32[768]{0:T(1024)S(1)} %add.351, f32[768]{0:T(1024)S(1)} %add.354, ...), channel_id=1, replica_groups=mesh['fsdp'=4,'context'=2,'tensor'=4] {'fsdp','context','tensor'}, use_global_device_ids=true, to_apply=%region_49.50 | all-reduce | flops 9984 | bytes 79872 | tf_op jit(solution)/shard_map/psum | solution.py:340
  1616.7 69.8 %all-reduce.17.cloned.1.call-done = (f32[256,128]{1,0:T(8,128)}, f32[128,4608]{1,0:T(8,128)}) async-done(((f32[256,128]{1,0:T(8,128)}, f32[128,4608]{1,0:T(8,128)}), (f32[256,128]{1,0:T(8,128)}, f32[128,4608]{1,0:T(8,128)})) %all-reduce.17.cloned.1.call-update) | async-done | bytes 2490384 | tf_op jit(solution)/shard_map/psum | solution.py:340
  (485 shorter events, 391.4 us)
Async XLA Ops:
  8.0 105.8 %all-gather.5.cloned.1.call-start = ((), (), s32[]{:S(2)}) async-start(), calls=%async_computation.6 | async-start | bytes 4718592 | tf_op jit(solution)/shard_map/all_gather | solution.py:193
  68.9 219.3 %all-reduce.13.cloned.1.call-start = ((), (), s32[]{:S(2)}) async-start(), calls=%async_computation.7 | async-start | bytes 6291456 | tf_op jit(solution)/shard_map/psum | solution.py:200
  219.7 125.3 %all-gather.11.cloned.1.call-start = ((), (), s32[]{:S(2)}) async-start(), calls=%async_computation.10 | async-start | bytes 4718592 | tf_op jit(solution)/shard_map/all_gather | solution.py:193
  299.8 221.0 %all-reduce.15.cloned.1.call-start = ((), (), s32[]{:S(2)}) async-start(), calls=%async_computation.11 | async-start | bytes 6291456 | tf_op jit(solution)/shard_map/psum | solution.py:200
  452.2 77.2 %all-gather.7.cloned.1.call-start = ((), (), s32[]{:S(2)}) async-start(), calls=%async_computation.8 | async-start | bytes 1474560 | tf_op jit(solution)/shard_map/all_gather | solution.py:138
  452.8 86.5 %all-gather.9.cloned.1.call-start = ((), (), s32[]{:S(2)}) async-start(), calls=%async_computation.9 | async-start | bytes 1474560 | tf_op jit(solution)/shard_map/all_gather | solution.py:140
  453.4 251.4 %all-reduce.21.cloned.1.call-start = ((), (), s32[]{:S(2)}) async-start(), calls=%async_computation.20 | async-start | bytes 12582912 | tf_op jit(solution)/shard_map/psum | solution.py:233
  453.4 251.3 %copy-start.52 = (f32[2048]{0:T(1024)}, f32[2048]{0:T(1024)S(1)}, u32[]{:S(2)}) copy-start(f32[2048]{0:T(1024)S(1)} %compare_convert_fusion.1) | copy-start | bytes 24580
  453.5 251.3 %copy-start.54 = (f32[2048]{0:T(1024)}, f32[2048]{0:T(1024)S(1)}, u32[]{:S(2)}) copy-start(f32[2048]{0:T(1024)S(1)} %compare_convert_fusion) | copy-start | bytes 24580
  453.5 123.6 %copy-start.91 = (f32[768]{0:T(1024)}, f32[768]{0:T(1024)S(1)}, u32[]{:S(2)}) copy-start(f32[768]{0:T(1024)S(1)} %convert_element_type.335) | copy-start | bytes 9220
  454.3 122.8 %copy-start.65 = (f32[2048]{0:T(1024)}, f32[2048]{0:T(1024)S(1)}, u32[]{:S(2)}) copy-start(f32[2048]{0:T(1024)S(1)} %broadcast_multiply_fusion.12) | copy-start | bytes 24580
  584.7 628.9 %reduce-scatter.19.cloned.1.call-start = ((), (), s32[]{:S(2)}) async-start(), calls=%async_computation.17 | async-start | bytes 491520
  586.1 128.5 %copy-start.19 = (f32[3,2048]{1,0:T(4,128)}, f32[3,2048]{1,0:T(4,128)S(1)}, u32[]{:S(2)}) copy-start(f32[3,2048]{1,0:T(4,128)S(1)} %log_add_fusion) | copy-start | bytes 73732
  820.4 394.9 %reduce-scatter.11.cloned.1.call-start = ((), (), s32[]{:S(2)}) async-start(), calls=%async_computation.13 | async-start | bytes 4718592 | tf_op jit(solution)/shard_map/reduce_scatter | solution.py:260
  926.5 291.9 %reduce-scatter.9.cloned.1.call-start = ((), (), s32[]{:S(2)}) async-start(), calls=%async_computation.12 | async-start | bytes 4718592 | tf_op jit(solution)/shard_map/reduce_scatter | solution.py:260
  1126.5 123.8 %reduce-scatter.17.cloned.1.call-start = ((), (), s32[]{:S(2)}) async-start(), calls=%async_computation.16 | async-start | bytes 1474560 | tf_op jit(solution)/shard_map/reduce_scatter | solution.py:317
  1141.4 108.9 %reduce-scatter.15.cloned.1.call-start = ((), (), s32[]{:S(2)}) async-start(), calls=%async_computation.15 | async-start | bytes 1474560 | tf_op jit(solution)/shard_map/reduce_scatter | solution.py:311
  1155.9 108.4 %reduce-scatter.13.cloned.1.call-start = ((), (), s32[]{:S(2)}) async-start(), calls=%async_computation.14 | async-start | bytes 1228800 | tf_op jit(solution)/shard_map/reduce_scatter | solution.py:308
  1237.4 63.7 %all-reduce.23.cloned.1.call-start = ((), (), s32[]{:S(2)}) async-start(), calls=%async_computation.21 | async-start | bytes 1867776 | tf_op jit(solution)/shard_map/psum | solution.py:322
  1264.3 261.9 %all-reduce.19.cloned.1.call-start = ((), (), s32[]{:S(2)}) async-start(), calls=%async_computation.19 | async-start | bytes 25165824 | tf_op jit(solution)/shard_map/psum | solution.py:211
  1293.7 232.4 %copy-start.56 = (f32[2048]{0:T(1024)S(1)}, f32[2048]{0:T(1024)}, u32[]{:S(2)}) copy-start(f32[2048]{0:T(1024)} %copy-done.54) | copy-start | bytes 24580
  1293.8 232.4 %copy-start.83 = (f32[768]{0:T(1024)S(1)}, f32[768]{0:T(1024)}, u32[]{:S(2)}) copy-start(f32[768]{0:T(1024)} %get-tuple-element.93) | copy-start | bytes 9220
  1293.8 232.4 %copy-start.86 = (f32[768]{0:T(1024)S(1)}, f32[768]{0:T(1024)}, u32[]{:S(2)}) copy-start(f32[768]{0:T(1024)} %get-tuple-element.96) | copy-start | bytes 9220
  1293.8 392.7 %all-reduce.17.cloned.1.call-start = ((), (), s32[]{:S(2)}) async-start(), calls=%async_computation.18 | async-start | bytes 4980736 | tf_op jit(solution)/shard_map/psum | solution.py:340
  (135 other events, 2466.6 us)
Sparse Core Ops, SparseCore 0:
  69.1 44.7 all-gather.4
  219.8 68.4 all-reduce.12
  299.9 45.0 all-gather.10
  452.3 68.4 all-reduce.14
  584.8 119.8 all-reduce.20
  1264.4 36.6 all-reduce.22
  1304.7 221.4 all-reduce.18
  1550.6 135.9 all-reduce.16
Sparse Core Ops, SparseCore 1:
  454.2 30.2 all-gather.6
  485.9 29.4 all-gather.8
  820.5 20.8 reduce-scatter.18
  926.6 43.5 reduce-scatter.10
  1126.6 43.4 reduce-scatter.8
  1172.5 29.2 reduce-scatter.16
  1204.0 27.8 reduce-scatter.14
  1237.5 26.7 reduce-scatter.12
where the time goes:
time: 1710 us; the launch traced here: 1700 us
  waiting for transfers between devices  614 us (36%)
  matrix products  573 us (34%)
  other arithmetic  354 us (21%)
  blocking collectives  80.5 us (5%)
  local copies, waits for them, and re-layouts  56.9 us (3%)
  between operations  18.7 us (1%)
    psum x1, waiting for transfers between devices, local(): lax.psum(product(activated_low, w_down).astype(jnp.bfloat16), 'tensor')  218 us
    convert_element_type x2, other arithmetic, attend_back(): grad_scores = (chances * (grad_chances - row_delta)).astype(jnp.bfloat16)  156 us
    psum x2, waiting for transfers between devices, local(): lax.psum(product(mixture_low, w_out).astype(jnp.bfloat16), 'tensor')  135 us
    dot_general x2, matrix products, attend_back(): jnp.einsum('qhd,khd->hqk', grad_mixture, values, preferred_element_type=j...  132 us
    psum x1, waiting for transfers between devices, local(): lax.psum(part_two.astype(jnp.bfloat16), 'tensor').astype(jnp.float32)  119 us
    dot_general x2, matrix products, scores_of(): jnp.einsum('qhd,khd->hqk', queries, key_rows, preferred_element_type=jnp....  75.4 us
    psum x1, waiting for transfers between devices, local(): lax.psum((grad_table, grad_ada_w, grad_ada_b, grad_gain_first, grad_gain_...  69.8 us
    dot_general x2, matrix products, attend(): jnp.einsum('hqk,khd->qhd', weights_low, values, preferred_element_type=jn...  68.5 us
  transfers between devices with their start and end apart: 16, of which 9 were waited for; matrix products, arithmetic and copies ran while one was open for 31% of the time, Pallas kernels for 0%

commit v1 on v0

--- a/solution.py
+++ b/solution.py
@@ -329,6 +329,7 @@
     grad_embedding = exact_against(grad_mod, ada_full)
     grad_before = silu_back(grad_embedding)[0]
     grad_table = exact_transposed(choose, grad_before)
+    cut_circles = lambda sample: lax.psum(lax.psum(sample, axis_name=("context", "tensor")), "fsdp")
     (
         grad_table,
         grad_ada_w,
@@ -337,7 +338,7 @@
         grad_gain_second,
         bias_up_full,
         grad_bias_down,
-    ) = lax.psum(
+    ) = cut_circles(
         (
             grad_table,
             grad_ada_w,
@@ -346,8 +347,7 @@
             grad_gain_second,
             bias_up_full,
             grad_bias_down * leader,
-        ),
-        ("fsdp", "context", "tensor"),
+        )
     )
     return (
         jnp.stack(results),

time: 1710 us -> 1680 us (0.982)
  waiting for transfers between devices: 614 us -> 591 us
    psum x1, waiting for transfers between devices: 218 us -> 173 us  [local(): lax.psum(product(activated_low, w_down).astype(jnp.bfloat16), 'tensor')]
    psum x1, waiting for transfers between devices: 5.22 us -> 38.9 us  [local(): lax.psum(grad_qkv.astype(jnp.bfloat16), 'context').astype(jnp.float32)]
    psum x1 -> x2, waiting for transfers between devices: 69.8 us -> 87.3 us  [the longest x1 61.9 us: local(): lax.psum(sample, axis_name=('context', 'tensor'))]
    psum x1 -> x2, blocking collectives: 41 us -> 45 us  [the longest x1 24.3 us: local(): lax.psum(sample, axis_name=('context', 'tensor'))]
  transfers between devices with their start and end apart: 16 -> 17, of which waited for: 9 -> 9; matrix products, arithmetic and copies ran while one was open for 31% -> 24% of each run, Pallas kernels for 0% -> 0%
where the time goes in v1:
time: 1680 us
  waiting for transfers between devices  591 us (35%)
  matrix products  572 us (34%)
  other arithmetic  350 us (21%)
  blocking collectives  84.8 us (5%)
  local copies, waits for them, and re-layouts  56.8 us (3%)
  between operations  19 us (1%)
    psum x1, waiting for transfers between devices, local(): lax.psum(product(activated_low, w_down).astype(jnp.bfloat16), 'tensor')  173 us
    convert_element_type x2, other arithmetic, attend_back(): grad_scores = (chances * (grad_chances - row_delta)).astype(jnp.bfloat16)  155 us
    psum x2, waiting for transfers between devices, local(): lax.psum(product(mixture_low, w_out).astype(jnp.bfloat16), 'tensor')  135 us
    dot_general x2, matrix products, attend_back(): jnp.einsum('qhd,khd->hqk', grad_mixture, values, preferred_element_type=j...  132 us
    psum x1, waiting for transfers between devices, local(): lax.psum(part_two.astype(jnp.bfloat16), 'tensor').astype(jnp.float32)  103 us
    dot_general x2, matrix products, scores_of(): jnp.einsum('qhd,khd->hqk', queries, key_rows, preferred_element_type=jnp....  75 us
    dot_general x2, matrix products, attend(): jnp.einsum('hqk,khd->qhd', weights_low, values, preferred_element_type=jn...  68.4 us
    dot_general x2, matrix products, local(): jnp.einsum('hqk,qhd->khd', chances_low, grad_mixture, preferred_element_t...  66.3 us
  transfers between devices with their start and end apart: 17, of which 9 were waited for; matrix products, arithmetic and copies ran while one was open for 24% of the time, Pallas kernels for 0%

profile of v1, /device:TPU:0, one launch (start us, length us, event | category | flops | bytes accessed | tf_op | source)
XLA Modules:
  0.0 1675.6 jit_solution(6222309052467722727)
XLA Ops:
  17.1 23.5 %all_gather.18 = bf16[768,576]{1,0:T(8,128)(2,1)S(1)} all-gather(bf16[192,576]{1,0:T(8,128)(2,1)S(1)} %copy-done.37), channel_id=1, replica_groups=mesh['fsdp'=4,'context'=2,'tensor'=4] {'fsdp'}, dimensions={0}, use_global_device_ids=true | all-gather | bytes 1105920 | tf_op jit(solution)/shard_map/all_gather | solution.py:137
  113.9 37.6 %fusion.185 = (f32[3,2048]{1,0:T(4,128)S(1)}, f32[3,2048,4096]{2,1,0:T(8,128)}) fusion(bf16[4096,2,3,64]{0,3,2,1:T(8,128)(2,1)} %bitcast.365, bf16[2048,3,32]{0,2,1:T(8,128)(2,1)S(1)} %get-tuple-element.159, bf16[2048,3,32]{0,2,1:T(8,128)(2,1)S(1)} %get-tuple-element.158, pred[2048,4096]{1,0:T(8,128)(4,1)} %broadcast_compare_fusion.1), kind=kOutput, calls=%fused_computation.352 | convolution fusion | flops 3298289664 | bytes 111435776 | tf_op jit(solution)/shard_map/qhd,khd->hqk/dot_general | solution.py:93
  151.5 31.0 %fusion = f32[3,2048]{1,0:T(4,128)S(1)} fusion(f32[3,2048,4096]{2,1,0:T(8,128)} %get-tuple-element.182, f32[3,2048]{1,0:T(4,128)S(1)} %get-tuple-element.181), kind=kLoop, calls=%fused_computation.12 | loop fusion | flops 50325504 | bytes 100712448 | tf_op jit(solution)/shard_map/reduce_sum | solution.py:102
  182.5 33.8 %fusion.119 = bf16[3,64,2048]{2,1,0:T(8,128)(2,1)S(1)} fusion(f32[3,2048,4096]{2,1,0:T(8,128)} %get-tuple-element.182, f32[3,2048]{1,0:T(4,128)S(1)} %fusion, f32[3,2048]{1,0:T(4,128)S(1)} %get-tuple-element.181, bf16[4096,2,3,64]{0,3,2,1:T(8,128)(2,1)} %bitcast.366), kind=kOutput, calls=%fused_computation.184 | convolution fusion | flops 3297116160 | bytes 103071744 | tf_op jit(solution)/shard_map/hqk,khd->qhd/dot_general | solution.py:104
  219.2 68.5 %all-reduce.16.cloned.1.call-done = bf16[2048,768]{1,0:T(8,128)(2,1)} async-done(((bf16[2048,768]{1,0:T(8,128)(2,1)}), bf16[2048,768]{1,0:T(8,128)(2,1)}) %all-reduce.16.cloned.1.call-update) | async-done | bytes 3145744 | tf_op jit(solution)/shard_map/psum | solution.py:200
  308.8 35.7 %all-gather.11.cloned.1.call-done = bf16[4096,384]{0,1:T(8,128)(2,1)} async-done(((bf16[2048,384]{0,1:T(8,128)(2,1)}), bf16[4096,384]{0,1:T(8,128)(2,1)}) %all-gather.11.cloned.1.call-update) | async-done | bytes 3145744 | tf_op jit(solution)/shard_map/all_gather | solution.py:193
  344.4 37.4 %fusion.186 = (f32[3,2048]{1,0:T(4,128)S(1)}, f32[3,2048,4096]{2,1,0:T(8,128)}) fusion(bf16[4096,2,3,64]{0,3,2,1:T(8,128)(2,1)} %bitcast.369, bf16[2048,3,32]{0,2,1:T(8,128)(2,1)S(1)} %get-tuple-element.155, bf16[2048,3,32]{0,2,1:T(8,128)(2,1)S(1)} %get-tuple-element.154, pred[2048,4096]{1,0:T(8,128)(4,1)} %broadcast_compare_fusion), kind=kOutput, calls=%fused_computation.353 | convolution fusion | flops 3298289664 | bytes 111435776 | tf_op jit(solution)/shard_map/qhd,khd->hqk/dot_general | solution.py:93
  381.9 31.0 %fusion.1 = f32[3,2048]{1,0:T(4,128)S(1)} fusion(f32[3,2048,4096]{2,1,0:T(8,128)} %get-tuple-element.184, f32[3,2048]{1,0:T(4,128)S(1)} %get-tuple-element.183), kind=kLoop, calls=%fused_computation.13 | loop fusion | flops 50325504 | bytes 100712448 | tf_op jit(solution)/shard_map/reduce_sum | solution.py:102
  412.9 34.6 %fusion.118 = bf16[3,64,2048]{2,1,0:T(8,128)(2,1)} fusion(f32[3,2048,4096]{2,1,0:T(8,128)} %get-tuple-element.184, f32[3,2048]{1,0:T(4,128)S(1)} %fusion.1, f32[3,2048]{1,0:T(4,128)S(1)} %get-tuple-element.183, bf16[4096,2,3,64]{0,3,2,1:T(8,128)(2,1)} %bitcast.370), kind=kOutput, calls=%fused_computation.183 | convolution fusion | flops 3297116160 | bytes 103071744 | tf_op jit(solution)/shard_map/hqk,khd->qhd/dot_general | solution.py:104
  453.8 66.5 %all-reduce.18.cloned.1.call-done = bf16[2048,768]{1,0:T(8,128)(2,1)} async-done(((bf16[2048,768]{1,0:T(8,128)(2,1)}), bf16[2048,768]{1,0:T(8,128)(2,1)}) %all-reduce.18.cloned.1.call-update) | async-done | bytes 3145744 | tf_op jit(solution)/shard_map/psum | solution.py:200
  600.6 103.4 %all-reduce.26.cloned.1.call-done = (bf16[2048,768]{1,0:T(8,128)(2,1)}, bf16[2048,768]{1,0:T(8,128)(2,1)}) async-done(((bf16[2048,768]{1,0:T(8,128)(2,1)}, bf16[2048,768]{1,0:T(8,128)(2,1)}), (bf16[2048,768]{1,0:T(8,128)(2,1)}, bf16[2048,768]{1,0:T(8,128)(2,1)})) %all-reduce.26.cloned.1.call-update) | async-done | bytes 6291472 | tf_op jit(solution)/shard_map/psum | solution.py:233
  713.8 33.7 %fusion.86 = bf16[4096,1,3,64]{0,3,2,1:T(8,128)(2,1)} fusion(bf16[2048,3,64]{0,2,1:T(8,128)(2,1)S(1)} %bitcast.363, f32[3,2048,4096]{2,1,0:T(8,128)} %get-tuple-element.184, f32[3,2048]{1,0:T(4,128)S(1)} %log_add_fusion), kind=kOutput, calls=%fused_computation.145 | convolution fusion | flops 3272343552 | bytes 103047168 | tf_op jit(solution)/shard_map/hqk,qhd->khd/dot_general | solution.py:253
  747.5 64.7 %multiply_reduce_fusion = (f32[3,2048]{1,0:T(4,128)S(1)}, f32[3,2048,4096]{2,1,0:T(8,128)}) fusion(f32[3,2048,4096]{2,1,0:T(8,128)} %get-tuple-element.184, f32[3,2048]{1,0:T(4,128)S(1)} %log_add_fusion, bf16[2048,3,64]{0,2,1:T(8,128)(2,1)S(1)} %bitcast.364, bf16[4096,2,3,64]{0,3,2,1:T(8,128)(2,1)} %bitcast.371), kind=kOutput, calls=%fused_computation.1 | convolution fusion | flops 3296716800 | bytes 203735040 | tf_op jit(solution)/shard_map/qhd,khd->hqk/dot_general | solution.py:111
  815.3 77.7 %multiply_convert_fusion = bf16[3,2048,4096]{2,1,0:T(8,128)(2,1)} fusion(f32[3,2048,4096]{2,1,0:T(8,128)} %get-tuple-element.191, f32[3,2048,4096]{2,1,0:T(8,128)} %get-tuple-element.184, f32[3,2048]{1,0:T(4,128)S(1)} %get-tuple-element.190, f32[3,2048]{1,0:T(4,128)S(1)} %log_add_fusion), kind=kLoop, calls=%fused_computation | loop fusion | flops 100663296 | bytes 251707392 | tf_op jit(solution)/shard_map/convert_element_type | solution.py:115
  917.9 67.6 %multiply_reduce_fusion.1 = (f32[3,2048]{1,0:T(4,128)S(1)}, f32[3,2048,4096]{2,1,0:T(8,128)}) fusion(f32[3,2048,4096]{2,1,0:T(8,128)} %get-tuple-element.182, f32[3,2048]{1,0:T(4,128)} %log_add_fusion.1, bf16[2048,3,64]{0,2,1:T(8,128)(2,1)S(1)} %bitcast.361, bf16[4096,2,3,64]{0,3,2,1:T(8,128)(2,1)} %bitcast.367), kind=kOutput, calls=%fused_computation.4 | convolution fusion | flops 3296716800 | bytes 203743232 | tf_op jit(solution)/shard_map/qhd,khd->hqk/dot_general | solution.py:111
  985.5 77.7 %multiply_convert_fusion.1 = bf16[3,2048,4096]{2,1,0:T(8,128)(2,1)} fusion(f32[3,2048,4096]{2,1,0:T(8,128)} %get-tuple-element.189, f32[3,2048,4096]{2,1,0:T(8,128)} %get-tuple-element.182, f32[3,2048]{1,0:T(4,128)S(1)} %get-tuple-element.188, f32[3,2048]{1,0:T(4,128)S(1)} %copy-done.19), kind=kLoop, calls=%fused_computation.3 | loop fusion | flops 100663296 | bytes 251707392 | tf_op jit(solution)/shard_map/convert_element_type | solution.py:115
  1083.4 32.6 %fusion.89 = bf16[4096,1,3,64]{0,3,2,1:T(8,128)(2,1)S(1)} fusion(bf16[2048,3,64]{0,2,1:T(8,128)(2,1)S(1)} %bitcast.362, f32[3,2048,4096]{2,1,0:T(8,128)} %get-tuple-element.182, f32[3,2048]{1,0:T(4,128)} %log_add_fusion.1), kind=kOutput, calls=%fused_computation.146 | convolution fusion | flops 3272343552 | bytes 103047168 | tf_op jit(solution)/shard_map/hqk,qhd->khd/dot_general | solution.py:253
  1118.0 23.1 %fusion.120 = f32[2048,3,64]{0,2,1:T(8,128)} fusion(bf16[3,2048,4096]{2,1,0:T(8,128)(2,1)} %multiply_convert_fusion, bf16[4096,2,3,64]{0,3,2,1:T(8,128)(2,1)} %bitcast.372), kind=kOutput, calls=%fused_computation.190 | convolution fusion | flops 3221618688 | bytes 53477376 | tf_op jit(solution)/shard_map/hqk,khd->qhd/dot_general | solution.py:246
  1141.1 22.2 %fusion.121 = f32[2048,3,64]{0,2,1:T(8,128)S(1)} fusion(bf16[3,2048,4096]{2,1,0:T(8,128)(2,1)} %multiply_convert_fusion.1, bf16[4096,2,3,64]{0,3,2,1:T(8,128)(2,1)} %bitcast.368), kind=kOutput, calls=%fused_computation.192 | convolution fusion | flops 3221618688 | bytes 53477376 | tf_op jit(solution)/shard_map/hqk,khd->qhd/dot_general | solution.py:246
  1259.1 172.6 %all-reduce.24.cloned.1.call-done = (bf16[2048,768]{1,0:T(8,128)(2,1)}, bf16[2048,768]{1,0:T(8,128)(2,1)}, bf16[2,2048,768]{1,0,2:T(2,128)(2,1)}) async-done(((bf16[2048,768]{1,0:T(8,128)(2,1)}, bf16[2048,768]{1,0:T(8,128)(2,1)}, bf16[2,2048,768]{1,0,2:T(2,128)(2,1)}), (bf16[2048,768]{1,0:T(8,128)(2,1)}, bf16[2048,768]{1,0:T(8,128)(2,1)}, bf16[2,2048,768]{1,0,2:T(2,128)(2,1)})) %all-reduce.24.cloned.1.call-update) | async-done | bytes 12582928 | tf_op jit(solution)/shard_map/psum | solution.py:211
  1457.8 61.9 %all-reduce.20.cloned.1.call-done = (f32[256,128]{1,0:T(8,128)}, f32[128,4608]{1,0:T(8,128)}) async-done(((f32[256,128]{1,0:T(8,128)}, f32[128,4608]{1,0:T(8,128)}), (f32[256,128]{1,0:T(8,128)}, f32[128,4608]{1,0:T(8,128)})) %all-reduce.20.cloned.1.call-update) | async-done | bytes 2490384 | tf_op jit(solution)/shard_map/psum | solution.py:332
  1521.2 38.9 %all-reduce.28.cloned.1.call-done = (bf16[192,576]{1,0:T(8,128)(2,1)}, bf16[192,192]{1,0:T(8,128)(2,1)}, bf16[192,768]{1,0:T(8,128)(2,1)}, bf16[768,192]{0,1:T(8,128)(2,1)}) async-done(((bf16[192,576]{1,0:T(8,128)(2,1)}, bf16[192,192]{1,0:T(8,128)(2,1)}, bf16[192,768]{1,0:T(8,128)(2,1)}, bf16[768,192]{0,1:T(8,128)(2,1)}), (bf16[192,576]{1,0:T(8,128)(2,1)}, bf16[192,192]{1,0:T(8,128)(2,1)}, ...) | async-done | bytes 884752 | tf_op jit(solution)/shard_map/psum | solution.py:322
  1586.5 24.3 %all-reduce.1 = (f32[4608]{0:T(1024)S(1)}, f32[768]{0:T(1024)S(1)}, f32[768]{0:T(1024)S(1)}, f32[3072]{0:T(1024)S(1)}, f32[768]{0:T(1024)S(1)}) all-reduce(f32[4608]{0:T(1024)S(1)} %reduce_sum.399, f32[768]{0:T(1024)S(1)} %add.365, f32[768]{0:T(1024)S(1)} %add.368, ...), channel_id=1, replica_groups=mesh['fsdp'=4,'context'=2,'tensor'=4] {'context','tensor'}, use_global_device_ids=true, to_apply=%region_51.52 | all-reduce | flops 9984 | bytes 79872 | tf_op jit(solution)/shard_map/psum | solution.py:332
  1637.7 25.4 %all-reduce.22.cloned.1.call-done = (f32[256,128]{1,0:T(8,128)}, f32[128,4608]{1,0:T(8,128)}) async-done(((f32[256,128]{1,0:T(8,128)}, f32[128,4608]{1,0:T(8,128)}), (f32[256,128]{1,0:T(8,128)}, f32[128,4608]{1,0:T(8,128)})) %all-reduce.22.cloned.1.call-update) | async-done | bytes 2490384 | tf_op jit(solution)/shard_map/psum | solution.py:332
  (500 shorter events, 431.1 us)
Async XLA Ops:
  8.0 105.8 %all-gather.5.cloned.1.call-start = ((), (), s32[]{:S(2)}) async-start(), calls=%async_computation.6 | async-start | bytes 4718592 | tf_op jit(solution)/shard_map/all_gather | solution.py:193
  68.9 218.8 %all-reduce.16.cloned.1.call-start = ((), (), s32[]{:S(2)}) async-start(), calls=%async_computation.7 | async-start | bytes 6291456 | tf_op jit(solution)/shard_map/psum | solution.py:200
  219.1 125.3 %all-gather.11.cloned.1.call-start = ((), (), s32[]{:S(2)}) async-start(), calls=%async_computation.10 | async-start | bytes 4718592 | tf_op jit(solution)/shard_map/all_gather | solution.py:193
  299.2 221.1 %all-reduce.18.cloned.1.call-start = ((), (), s32[]{:S(2)}) async-start(), calls=%async_computation.11 | async-start | bytes 6291456 | tf_op jit(solution)/shard_map/psum | solution.py:200
  451.7 77.2 %all-gather.7.cloned.1.call-start = ((), (), s32[]{:S(2)}) async-start(), calls=%async_computation.8 | async-start | bytes 1474560 | tf_op jit(solution)/shard_map/all_gather | solution.py:138
  452.3 86.5 %all-gather.9.cloned.1.call-start = ((), (), s32[]{:S(2)}) async-start(), calls=%async_computation.9 | async-start | bytes 1474560 | tf_op jit(solution)/shard_map/all_gather | solution.py:140
  452.8 251.1 %all-reduce.26.cloned.1.call-start = ((), (), s32[]{:S(2)}) async-start(), calls=%async_computation.21 | async-start | bytes 12582912 | tf_op jit(solution)/shard_map/psum | solution.py:233
  452.9 251.1 %copy-start.51 = (f32[2048]{0:T(1024)}, f32[2048]{0:T(1024)S(1)}, u32[]{:S(2)}) copy-start(f32[2048]{0:T(1024)S(1)} %compare_convert_fusion.1) | copy-start | bytes 24580
  452.9 251.0 %copy-start.53 = (f32[2048]{0:T(1024)}, f32[2048]{0:T(1024)S(1)}, u32[]{:S(2)}) copy-start(f32[2048]{0:T(1024)S(1)} %compare_convert_fusion) | copy-start | bytes 24580
  453.8 138.3 %copy-start.119 = (f32[768]{0:T(1024)}, f32[768]{0:T(1024)S(1)}, u32[]{:S(2)}) copy-start(f32[768]{0:T(1024)S(1)} %dynamic-slice_convert_fusion) | copy-start | bytes 9220
  583.9 579.4 %reduce-scatter.11.cloned.1.call-start = ((), (), s32[]{:S(2)}) async-start(), calls=%async_computation.13 | async-start | bytes 4718592 | tf_op jit(solution)/shard_map/reduce_scatter | solution.py:260
  917.9 248.6 %reduce-scatter.9.cloned.1.call-start = ((), (), s32[]{:S(2)}) async-start(), calls=%async_computation.12 | async-start | bytes 4718592 | tf_op jit(solution)/shard_map/reduce_scatter | solution.py:260
  1117.9 313.8 %all-reduce.24.cloned.1.call-start = ((), (), s32[]{:S(2)}) async-start(), calls=%async_computation.20 | async-start | bytes 25165824 | tf_op jit(solution)/shard_map/psum | solution.py:211
  1210.0 246.1 %reduce-scatter.19.cloned.1.call-start = ((), (), s32[]{:S(2)}) async-start(), calls=%async_computation.17 | async-start | bytes 491520
  1220.4 237.3 %reduce-scatter.17.cloned.1.call-start = ((), (), s32[]{:S(2)}) async-start(), calls=%async_computation.16 | async-start | bytes 1474560 | tf_op jit(solution)/shard_map/reduce_scatter | solution.py:317
  1230.3 227.4 %reduce-scatter.15.cloned.1.call-start = ((), (), s32[]{:S(2)}) async-start(), calls=%async_computation.15 | async-start | bytes 1474560 | tf_op jit(solution)/shard_map/reduce_scatter | solution.py:311
  1244.9 212.9 %reduce-scatter.13.cloned.1.call-start = ((), (), s32[]{:S(2)}) async-start(), calls=%async_computation.14 | async-start | bytes 1228800 | tf_op jit(solution)/shard_map/reduce_scatter | solution.py:308
  1252.5 179.2 %copy-start.55 = (f32[2048]{0:T(1024)S(1)}, f32[2048]{0:T(1024)}, u32[]{:S(2)}) copy-start(f32[2048]{0:T(1024)} %copy-done.53) | copy-start | bytes 24580
  1252.5 179.2 %copy-start.83 = (f32[768]{0:T(1024)S(1)}, f32[768]{0:T(1024)}, u32[]{:S(2)}) copy-start(f32[768]{0:T(1024)} %convert_element_type.341) | copy-start | bytes 9220
  1252.5 179.2 %copy-start.86 = (f32[768]{0:T(1024)S(1)}, f32[768]{0:T(1024)}, u32[]{:S(2)}) copy-start(f32[768]{0:T(1024)} %get-tuple-element.93) | copy-start | bytes 9220
  1252.5 179.2 %copy-start.89 = (f32[768]{0:T(1024)S(1)}, f32[768]{0:T(1024)}, u32[]{:S(2)}) copy-start(f32[768]{0:T(1024)} %get-tuple-element.96) | copy-start | bytes 9220
  1258.9 260.8 %all-reduce.20.cloned.1.call-start = ((), (), s32[]{:S(2)}) async-start(), calls=%async_computation.18 | async-start | bytes 4980736 | tf_op jit(solution)/shard_map/psum | solution.py:332
  1455.9 104.3 %all-reduce.28.cloned.1.call-start = ((), (), s32[]{:S(2)}) async-start(), calls=%async_computation.22 | async-start | bytes 1867776 | tf_op jit(solution)/shard_map/psum | solution.py:322
  1457.8 205.3 %all-reduce.22.cloned.1.call-start = ((), (), s32[]{:S(2)}) async-start(), calls=%async_computation.19 | async-start | bytes 4980736 | tf_op jit(solution)/shard_map/psum | solution.py:332
  (142 other events, 2730.5 us)
Sparse Core Ops, SparseCore 0:
  69.0 44.7 all-gather.4
  219.2 68.4 all-reduce.15
  299.4 45.0 all-gather.10
  451.8 68.4 all-reduce.17
  584.1 119.8 all-reduce.25
  918.0 43.5 reduce-scatter.10
  1118.0 43.5 reduce-scatter.8
  1210.1 221.5 all-reduce.23
Sparse Core Ops, SparseCore 1:
  453.7 30.2 all-gather.6
  485.4 29.4 all-gather.8
  1220.5 20.8 reduce-scatter.18
  1243.7 27.3 reduce-scatter.16
  1273.5 27.8 reduce-scatter.14
  1303.8 24.7 reduce-scatter.12
  1455.9 63.7 all-reduce.19
  1522.8 37.3 all-reduce.27
  1562.5 100.5 all-reduce.21
